TPU v7x, 128 devices: a whole 4x4x4 slice. The times are simulated.
128 devices in a mesh: dp: 16 (over x_lo, z, core), tensor: 8 (over y, x_hi).
Axes of the slice: x: 4 (x_hi: 2, x_lo: 2; x = x_hi * 2 + x_lo), y: 4, z: 4, core: 2. Of those that a mesh axis runs over, the one named last changes fastest.
Arguments:
- queries: bfloat16 [49152, 1024], P('dp', 'tensor'), may hold values from -80 to 80
- keys: bfloat16 [49152, 128], P('dp'), may hold values from -6 to 6
- values: bfloat16 [49152, 128], P('dp'), may hold values from -6 to 6
- dout: bfloat16 [49152, 1024], P('dp', 'tensor'), may hold values from -6 to 6
- offsets: int32 [8], replicated, may hold values from 0 to 2047
- lengths: int32 [16], P('dp'), may hold values from 256 to 1024
Outputs:
- dq: bfloat16 [49152, 1024], P('dp', 'tensor')
- dk: bfloat16 [49152, 128], P('dp')
- dv: bfloat16 [49152, 128], P('dp')
All inputs are finite; a program needn't handle non-finite values.
Results may differ from a plain program's by a relative error of at most 0.015.
Values may be sent and summed in bfloat16 or wider, within the bound.
A program may use at most 128 MiB of HBM per device.

v0:
```python
import functools

import jax
import jax.numpy as jnp
from jax import lax
from jax.experimental import pallas as pl
from jax.experimental.pallas import tpu as pltpu
from jax.sharding import PartitionSpec as P

MESH = pl.DeviceIdType.MESH
f32 = jnp.float32
bf = jnp.bfloat16

PH = 2048
R = 1024
DH = 128
KEYS = 2 * PH + R
BQ, BK = 256, 512
RG = 16
T = BK // 128
NT = 8
FT = 2 * DH // NT
NPC = 4
PC = PH // NPC
HP = PH // 2
XR = 768
ROWS = PH + R
NEG = -1e30
EARLY = (3,)
SCALE = 1.0 / DH**0.5
CC = SCALE * 1.4426950408889634


def dot_nt(a, b):
    return lax.dot_general(a, b, (((1,), (1,)), ((), ())), preferred_element_type=f32)


def dot_nn(a, b):
    return jnp.dot(a, b, preferred_element_type=f32)


def kernel(
    offs, lens, q, kin, vin, do, dq, dk, dv,
    k, v, dkT, dvT, S, E, DP0, DP1, mx, mb, la, ta, rl, dl, dqa, dom, qT, dT, bias,
    qa, dqx, sb, rb, rr, ga,
    kv_s, kv_r, p_s, p_r, r_s, r_r, g_s, g_r, x_s, x_r,
):
    d = lax.axis_index("dp")
    t = lax.axis_index("tensor")
    half = lax.axis_size("dp") // 2
    side = lax.div(d, half)
    pair = lax.rem(d, half)
    offset = offs[pair]
    length = lens[0]

    def peer(b, a):
        return (lax.rem(side + b, 2) * half + pair, lax.rem(t + a, NT))

    barrier = pltpu.get_barrier_semaphore()
    for i in range(1, 2 * NT):
        pl.semaphore_signal(barrier, inc=1, device_id=peer(i // NT, i % NT), device_id_type=MESH)
    pl.semaphore_wait(barrier, 2 * NT - 1)

    flip = t + 1 - 2 * lax.rem(t, 2)
    kv = []
    for h in range(2):
        dst = (lax.rem(side + 1, 2) * half + pair, t if h == 0 else flip)
        for i, (src, to) in enumerate(((kin, k), (vin, v))):
            rows = pl.ds(pl.multiple_of(side * PH + h * HP, HP), HP)
            c = pltpu.make_async_remote_copy(
                src_ref=src.at[pl.ds(h * HP, HP)], dst_ref=to.at[rows],
                send_sem=kv_s.at[2 * h + i], recv_sem=kv_r.at[2 * h + i],
                device_id=dst, device_id_type=MESH,
            )
            c.start()
            kv.append(c)

    over = [
        pltpu.make_async_remote_copy(
            src_ref=src.at[pl.ds(PH - XR, XR)], dst_ref=to.at[pl.ds(ROWS, XR)],
            send_sem=x_s.at[i], recv_sem=x_r.at[i], device_id=peer(1, 0), device_id_type=MESH,
        )
        for i, (src, to) in enumerate(((q, qa), (do, dom)))
    ]
    back = pltpu.make_async_remote_copy(
        src_ref=dqx, dst_ref=dq.at[pl.ds(PH - XR, XR)],
        send_sem=x_s.at[2], recv_sem=x_r.at[2], device_id=peer(1, 0), device_id_type=MESH,
    )

    @pl.when(side == 1)
    def _():
        for c in over:
            c.start()

    own = pl.ds(pl.multiple_of(side * PH, PH), PH)
    qa[:ROWS, :] = q[...]
    k[own, :] = kin[:PH, :]
    v[own, :] = vin[:PH, :]
    k[2 * PH :, :] = kin[PH:, :]
    v[2 * PH :, :] = vin[PH:, :]
    dom[:PH, :] = do[:PH, :]
    row = lax.broadcasted_iota(jnp.int32, (R, DH), 0)
    dom[PH:ROWS, :] = jnp.where(row < length, do[PH:, :], jnp.zeros((R, DH), bf))
    kp = lax.broadcasted_iota(jnp.int32, (8, KEYS), 1)
    bias[...] = jnp.where(kp >= offset, 0.0, NEG).astype(f32)
    dkT[...] = jnp.zeros_like(dkT)
    dvT[...] = jnp.zeros_like(dvT)
    for c in kv:
        c.wait_recv()

    NR, NP = R // BQ, PH // BQ
    NX = XR // BQ
    NB = NR + NP + NX - 2 * NX * side
    DPS = (DP0, DP1)

    def info(j):
        resp = j < NR
        extra = (side == 0) & (j >= NR) & (j < NR + NX)
        b = NB - 1 - j
        x = NR + NX - 1 - j
        row0 = jnp.where(resp, PH + (NR - 1 - j) * BQ, jnp.where(extra, ROWS + x * BQ, b * BQ))
        pos0 = jnp.where(resp, PH + row0, jnp.where(extra, 2 * PH - XR + x * BQ, side * PH + row0))
        n = jnp.where(j < NB, lax.div(pos0 + BQ - 1, BK) + 1, 0)
        return pl.multiple_of(jnp.maximum(row0, 0), BQ), pos0, n

    def ks(c):
        return pl.ds(pl.multiple_of(c * BK, BK), BK)

    def scores(slot, row0, pos0, c, masked):
        DP = DPS[slot]
        s = dot_nt(qa[pl.ds(row0, BQ), :], k[ks(c), :])
        dp = dot_nt(dom[pl.ds(row0, BQ), :], v[ks(c), :])
        if masked:
            cols = lax.broadcasted_iota(jnp.int32, (RG, 128), 1)
        for r in range(0, BQ, RG):
            m = mx[r : r + RG, :]
            for i in range(T):
                st = s[r : r + RG, i * 128 : (i + 1) * 128]
                if masked:
                    rows = lax.broadcasted_iota(jnp.int32, (RG, 128), 0) + (pos0 - c * BK + r)
                    ct = cols + i * 128
                    ok = (ct < rows) & (ct + c * BK >= offset) | (ct == rows)
                    st = jnp.where(ok, st, NEG)
                else:
                    st = st + bias[0:1, pl.ds(pl.multiple_of(c * BK + i * 128, 128), 128)]
                S[c * T + i, r : r + RG, :] = st
                m = jnp.maximum(m, st)
                DP[c * T + i, r : r + RG, :] = dp[r : r + RG, i * 128 : (i + 1) * 128]
            mx[r : r + RG, :] = m

    def expo(slot, c):
        DP = DPS[slot]
        for r in range(0, BQ, RG):
            l, tt, m = la[r : r + RG, :], ta[r : r + RG, :], mb[r : r + RG, :]
            for i in range(T):
                e = jnp.exp2(S[c * T + i, r : r + RG, :] * CC - m)
                l = l + e
                tt = tt + e * DP[c * T + i, r : r + RG, :]
                E[c * T + i, r : r + RG, :] = e
            la[r : r + RG, :] = l
            ta[r : r + RG, :] = tt

    def grads_in(slot, c):
        DP = DPS[slot]
        ps, xs = [], []
        for r in range(0, BQ, RG):
            rv, dd = rl[r : r + RG, :], dl[r : r + RG, :]
            pr, xr = [], []
            for i in range(T):
                p = E[c * T + i, r : r + RG, :] * rv
                x = p * (DP[c * T + i, r : r + RG, :] - dd)
                pr.append(p.astype(bf))
                xr.append(x.astype(bf))
            ps.append(jnp.concatenate(pr, 1))
            xs.append(jnp.concatenate(xr, 1))
        return jnp.concatenate(ps, 0), jnp.concatenate(xs, 0)

    def grads_out(c, p, x):
        gv = dot_nn(dT[...], p)
        gk = dot_nn(qT[...], x)
        for i in range(T):
            dvT[c * T + i] += gv[:, i * 128 : (i + 1) * 128]
            dkT[c * T + i] += gk[:, i * 128 : (i + 1) * 128]
        dqa[...] += dot_nn(x, k[ks(c), :])

    def row_max():
        mb[...] = jnp.broadcast_to(jnp.max(mx[...], axis=1, keepdims=True) * CC, (BQ, 128))
        mx[...] = jnp.full((BQ, 128), NEG, f32)

    def row_sums():
        inv = 1.0 / jnp.sum(la[...], axis=1, keepdims=True)
        rl[...] = jnp.broadcast_to(inv, (BQ, 128))
        dl[...] = jnp.broadcast_to(jnp.sum(ta[...], axis=1, keepdims=True) * inv, (BQ, 128))
        la[...] = jnp.zeros((BQ, 128), f32)
        ta[...] = jnp.zeros((BQ, 128), f32)

    def turn(row):
        qT[...] = qa[pl.ds(row, BQ), :].T
        dT[...] = dom[pl.ds(row, BQ), :].T
        dqa[...] = jnp.zeros((BQ, DH), f32)

    def loop(lo, hi, f):
        def body(c, _):
            f(c)
            return 0

        lax.fori_loop(lo, hi, body, 0)

    def feats(a):
        return pl.ds(pl.multiple_of(lax.rem(t + a, NT) * FT, FT), FT)

    def prompt_copy(b, a, h):
        cols = pl.ds(pl.multiple_of(lax.rem(side + b, 2) * PH + h * PC, PC), PC)
        i = b * NT + a
        return pltpu.make_async_remote_copy(
            src_ref=sb.at[feats(a), cols], dst_ref=rb.at[i, :, pl.ds(h * PC, PC)],
            send_sem=p_s.at[h, i], recv_sem=p_r.at[h, i],
            device_id=peer(b, a), device_id_type=MESH,
        )

    def resp_copy(a):
        return pltpu.make_async_remote_copy(
            src_ref=sb.at[feats(a), pl.ds(2 * PH, R)], dst_ref=rr.at[a],
            send_sem=r_s.at[a], recv_sem=r_r.at[a],
            device_id=peer(0, a), device_id_type=MESH,
        )

    def gather(piece, a):
        cols = pl.ds(piece * PC, PC if piece < NPC else R)
        return pltpu.make_async_remote_copy(
            src_ref=ga.at[feats(0), cols], dst_ref=ga.at[feats(0), cols],
            send_sem=g_s.at[piece, a], recv_sem=g_r.at[piece, a],
            device_id=peer(0, a), device_id_type=MESH,
        )

    def pack(c0, tiles):
        def one(i):
            c = c0 + i
            cols = pl.ds(pl.multiple_of(c * 128, 128), 128)
            sb[:DH, cols] = (dkT[c] * SCALE).astype(bf)
            sb[DH:, cols] = dvT[c].astype(bf)

        loop(0, tiles, one)

    HT = PC // 128

    def send_resp():
        pack(2 * PH // 128, R // 128)
        for a in range(1, NT):
            resp_copy(a).start()

    def send_prompt(b, h):
        pack(lax.rem(side + b, 2) * NPC * HT + h * HT, HT)
        for a in range(0 if b else 1, NT):
            prompt_copy(b, a, h).start()

    def finish_resp():
        for a in range(1, NT):
            resp_copy(a).wait_recv()
        for i in range(R // 128):
            cols = slice(i * 128, (i + 1) * 128)
            total = sb[feats(0), 2 * PH + i * 128 : 2 * PH + (i + 1) * 128].astype(f32)
            for a in range(1, NT):
                total = total + rr[a, :, cols].astype(f32)
            ga[feats(0), PH + i * 128 : PH + (i + 1) * 128] = total.astype(bf)
        for a in range(1, NT):
            gather(NPC, a).start()

    def finish_prompt(h):
        for i in range(1, 2 * NT):
            prompt_copy(i // NT, i % NT, h).wait_recv()
        for c in range(HT):
            cols = slice(h * PC + c * 128, h * PC + (c + 1) * 128)
            mine = pl.ds(pl.multiple_of(side * PH + h * PC + c * 128, 128), 128)
            total = sb[feats(0), mine].astype(f32)
            for i in range(1, 2 * NT):
                total = total + rb[i, :, cols].astype(f32)
            ga[feats(0), cols] = total.astype(bf)
        for a in range(1, NT):
            gather(h, a).start()

    mx[...] = jnp.full((BQ, 128), NEG, f32)
    la[...] = jnp.zeros((BQ, 128), f32)
    ta[...] = jnp.zeros((BQ, 128), f32)
    row_a, pos_a, na = info(jnp.int32(0))
    row_b, pos_b, nb = info(jnp.int32(1))
    loop(0, na - 1, lambda c: scores(0, row_a, pos_a, c, False))
    scores(0, row_a, pos_a, na - 1, True)
    row_max()

    def first(c, masked=False):
        expo(0, c)
        scores(1, row_b, pos_b, c, masked)

    loop(0, nb - 1, first)
    first(nb - 1, True)
    loop(nb, na, lambda c: expo(0, c))
    row_sums()
    row_max()
    turn(row_a)

    def block(j, slot):
        r0, _, n0 = info(j)
        r1, _, n1 = info(j + 1)
        r2, p2, n2 = info(j + 2)

        def three(c, masked=False):
            p, x = grads_in(slot, c)
            expo(1 - slot, c)
            scores(slot, r2, p2, c, masked)
            grads_out(c, p, x)

        def two_of(c):
            p, x = grads_in(slot, c)
            expo(1 - slot, c)
            grads_out(c, p, x)

        def one_of(c):
            grads_out(c, *grads_in(slot, c))

        loop(0, n2 - 1, three)

        @pl.when(n2 > 0)
        def _():
            three(n2 - 1, True)

        loop(n2, n1, two_of)
        loop(n1, n0, one_of)
        @pl.when((r0 < ROWS) & (n0 > 0))
        def _():
            dq[pl.ds(r0, BQ), :] = (dqa[...] * SCALE).astype(bf)

        @pl.when(r0 >= ROWS)
        def _():
            dqx[pl.ds(pl.multiple_of(r0 - ROWS, BQ), BQ), :] = (dqa[...] * SCALE).astype(bf)


        @pl.when(n1 > 0)
        def _():
            row_sums()
            row_max()
            turn(r1)

        @pl.when(j == NR - 1)
        def _():
            send_resp()

            @pl.when(side == 1)
            def _():
                for h in range(-((NX - NP) // 2), NPC):
                    send_prompt(0, h)

        @pl.when((side == 0) & (j == NR + NX - 1))
        def _():
            back.start()
            for h in range(NPC - 1, -1, -1):
                send_prompt(1, h)

        @pl.when(j == NR + 1)
        def _():
            finish_resp()

        b = NB - 1 - j
        for h in range(1, NPC):

            @pl.when((b == 2 * h) & (j >= NR + NX - NX * side))
            def _():
                send_prompt(0, h)

        @pl.when((side == 0) & (b == 1))
        def _():
            for h in EARLY:
                finish_prompt(h)

    def two(i):
        @pl.when((side == 0) & (i == 1))
        def _():
            for c in over:
                c.wait_recv()

        block(2 * i, 0)
        block(2 * i + 1, 1)

    loop(0, lax.div(NB + 1, 2), two)

    @pl.when(side == 1)
    def _():
        for h in range(NPC - 1, -1, -1):
            send_prompt(1, h)

    send_prompt(0, 0)

    @pl.when(side == 1)
    def _():
        for h in EARLY:
            finish_prompt(h)

    for h in range(NPC - 1, -1, -1):
        if h not in EARLY:
            finish_prompt(h)

    @pl.when(side == 0)
    def _():
        back.wait_send()

    @pl.when(side == 1)
    def _():
        back.wait_recv()
        for c in over:
            c.wait_send()

    for c in kv:
        c.wait_send()
    for i in range(1, 2 * NT):
        for h in range(NPC):
            prompt_copy(i // NT, i % NT, h).wait_send()
    for a in range(1, NT):
        resp_copy(a).wait_send()
    for piece in range(NPC, -1, -1):
        for a in range(1, NT):
            gather(piece, a).wait()
        for c in range(piece * PC, ROWS if piece == NPC else (piece + 1) * PC, 256):
            dk[c : c + 256, :] = ga[:DH, c : c + 256].T
            dv[c : c + 256, :] = ga[DH:, c : c + 256].T


def per_device(queries, keys, values, dout, offsets, lengths):
    V = pl.BlockSpec(memory_space=pltpu.VMEM)
    SM = pl.BlockSpec(memory_space=pltpu.SMEM)
    D = pltpu.SemaphoreType.DMA
    big = pltpu.VMEM((KEYS // 128, BQ, 128), f32)
    acc = pltpu.VMEM((KEYS // 128, DH, 128), f32)
    stat = pltpu.VMEM((BQ, 128), f32)
    return tuple(
        pl.pallas_call(
            kernel,
            out_shape=[jax.ShapeDtypeStruct((ROWS, DH), bf)] * 3,
            in_specs=[SM, SM, V, V, V, V],
            out_specs=[V, V, V],
            scratch_shapes=[
                pltpu.VMEM((KEYS, DH), bf), pltpu.VMEM((KEYS, DH), bf),
                acc, acc, big, big, big, big,
                stat, stat, stat, stat, stat, stat,
                pltpu.VMEM((BQ, DH), f32), pltpu.VMEM((ROWS + XR, DH), bf),
                pltpu.VMEM((DH, BQ), bf), pltpu.VMEM((DH, BQ), bf),
                pltpu.VMEM((8, KEYS), f32),
                pltpu.VMEM((ROWS + XR, DH), bf), pltpu.VMEM((XR, DH), bf),
                pltpu.VMEM((2 * DH, KEYS), bf), pltpu.VMEM((2 * NT, FT, PH), bf),
                pltpu.VMEM((NT, FT, R), bf), pltpu.VMEM((2 * DH, ROWS), bf),
                D((4,)), D((4,)), D((NPC, 2 * NT)), D((NPC, 2 * NT)), D((NT,)), D((NT,)),
                D((NPC + 1, NT)), D((NPC + 1, NT)), D((3,)), D((3,)),
            ],
            compiler_params=pltpu.CompilerParams(
                collective_id=0, has_side_effects=True, vmem_limit_bytes=60 * 2**20
            ),
        )(offsets, lengths, queries, keys, values, dout)
    )


def solution(mesh):
    return jax.shard_map(
        per_device,
        mesh=mesh,
        in_specs=(P("dp", "tensor"), P("dp", None), P("dp", None), P("dp", "tensor"), P(), P("dp")),
        out_specs=(P("dp", "tensor"), P("dp", None), P("dp", None)),
        check_vma=False,
    )
```

profile of v0, /device:TPU:0, one launch (start us, length us, event | category | flops | bytes accessed | tf_op | source)
XLA Modules:
  0.0 113.2 jit_solution(10920183217391228031)
XLA Ops:
  1.3 107.4 %shard_map.85 = (bf16[3072,128]{1,0:T(8,128)(2,1)}, bf16[3072,128]{1,0:T(8,128)(2,1)}, bf16[3072,128]{1,0:T(8,128)(2,1)}) custom-call(s32[8]{0:T(128)} %offs.1, s32[1]{0:T(128)S(6)} %copy.12.lens, bf16[3072,128]{1,0:T(8,128)(2,1)} %q.1, bf16[3072,128]{1,0:T(8,128)(2,1)} %kin.1, bf16[3072,128]{1,0:T(8,128)(2,1)} %vin.1, bf16[3072,128]{1,0:T(8,128)(2,1)} %do.1), custom_call_target="tpu_custom_call" | custom-call | tf_op jit(solution)/shard_map/pallas_call | solution.py:435
  108.7 0.0 copy-start.1
  108.7 2.1 %copy.13 = bf16[3072,128]{1,0:T(8,128)(2,1)} copy(bf16[3072,128]{1,0:T(8,128)(2,1)} %get-tuple-element.6) | data formatting | bytes 1572864
  110.9 0.0 copy-done.1
  110.9 0.0 copy-start
  110.9 0.9 copy.14
  111.7 0.5 copy-done
  112.3 0.9 copy.15
Async XLA Ops:
  108.7 2.1 %copy-start.1 = (bf16[3072,128]{1,0:T(8,128)(2,1)S(1)}, bf16[3072,128]{1,0:T(8,128)(2,1)}, u32[]{:S(2)}) copy-start(bf16[3072,128]{1,0:T(8,128)(2,1)} %get-tuple-element.7) | copy-start | bytes 2359300
  110.9 1.4 %copy-start = (bf16[3072,128]{1,0:T(8,128)(2,1)S(1)}, bf16[3072,128]{1,0:T(8,128)(2,1)}, u32[]{:S(2)}) copy-start(bf16[3072,128]{1,0:T(8,128)(2,1)} %get-tuple-element.8) | copy-start | bytes 2359300
where the time goes:
time: 113 us
  Pallas kernels  107 us (95%)
  local copies, waits for them, and re-layouts  4.44 us (4%)
  between operations  1.3 us (1%)
    pallas_call x1, Pallas kernels, per_device(): pl.pallas_call(kernel, out_shape=[jax.ShapeDtypeStruct((ROWS, DH), bf)] *...  107 us
    unnamed x7, local copies, waits for them, and re-layouts  4.44 us

commit v1 on v0

--- a/solution.py
+++ b/solution.py
@@ -43,7 +43,7 @@
     offs, lens, q, kin, vin, do, dq, dk, dv,
     k, v, dkT, dvT, S, E, DP0, DP1, mx, mb, la, ta, rl, dl, dqa, dom, qT, dT, bias,
     qa, dqx, sb, rb, rr, ga,
-    kv_s, kv_r, p_s, p_r, r_s, r_r, g_s, g_r, x_s, x_r,
+    kv_s, kv_r, p_s, p_r, r_s, r_r, g_s, g_r, x_s, x_r, l_s,
 ):
     d = lax.axis_index("dp")
     t = lax.axis_index("tensor")
@@ -55,6 +55,18 @@
 
     def peer(b, a):
         return (lax.rem(side + b, 2) * half + pair, lax.rem(t + a, NT))
+
+    own = pl.ds(pl.multiple_of(side * PH, PH), PH)
+    loads = [
+        pltpu.make_async_copy(src, dst, l_s.at[i])
+        for i, (src, dst) in enumerate((
+            (kin.at[pl.ds(0, PH)], k.at[own]), (kin.at[pl.ds(PH, R)], k.at[pl.ds(2 * PH, R)]),
+            (vin.at[pl.ds(0, PH)], v.at[own]), (vin.at[pl.ds(PH, R)], v.at[pl.ds(2 * PH, R)]),
+            (q, qa.at[pl.ds(0, ROWS)]), (do, dom.at[pl.ds(0, ROWS)]),
+        ))
+    ]
+    for c in loads:
+        c.start()
 
     barrier = pltpu.get_barrier_semaphore()
     for i in range(1, 2 * NT):
@@ -92,21 +104,14 @@
         for c in over:
             c.start()
 
-    own = pl.ds(pl.multiple_of(side * PH, PH), PH)
-    qa[:ROWS, :] = q[...]
-    k[own, :] = kin[:PH, :]
-    v[own, :] = vin[:PH, :]
-    k[2 * PH :, :] = kin[PH:, :]
-    v[2 * PH :, :] = vin[PH:, :]
-    dom[:PH, :] = do[:PH, :]
-    row = lax.broadcasted_iota(jnp.int32, (R, DH), 0)
-    dom[PH:ROWS, :] = jnp.where(row < length, do[PH:, :], jnp.zeros((R, DH), bf))
     kp = lax.broadcasted_iota(jnp.int32, (8, KEYS), 1)
     bias[...] = jnp.where(kp >= offset, 0.0, NEG).astype(f32)
     dkT[...] = jnp.zeros_like(dkT)
     dvT[...] = jnp.zeros_like(dvT)
-    for c in kv:
-        c.wait_recv()
+    for c in loads:
+        c.wait()
+    row = lax.broadcasted_iota(jnp.int32, (R, DH), 0)
+    dom[PH:ROWS, :] = jnp.where(row < length, dom[PH:ROWS, :], jnp.zeros((R, DH), bf))
 
     NR, NP = R // BQ, PH // BQ
     NX = XR // BQ
@@ -284,8 +289,13 @@
     ta[...] = jnp.zeros((BQ, 128), f32)
     row_a, pos_a, na = info(jnp.int32(0))
     row_b, pos_b, nb = info(jnp.int32(1))
-    loop(0, na - 1, lambda c: scores(0, row_a, pos_a, c, False))
+    PB = PH // BK
+    loop(side * PB, side * PB + PB, lambda c: scores(0, row_a, pos_a, c, False))
+    loop(2 * PB, na - 1, lambda c: scores(0, row_a, pos_a, c, False))
     scores(0, row_a, pos_a, na - 1, True)
+    for c in kv:
+        c.wait_recv()
+    loop(PB - side * PB, 2 * PB - side * PB, lambda c: scores(0, row_a, pos_a, c, False))
     row_max()
 
     def first(c, masked=False):
@@ -392,6 +402,9 @@
 
     @pl.when(side == 1)
     def _():
+        for h in range(NPC):
+            for a in range(NT):
+                prompt_copy(1, a, h).wait_send()
         for h in EARLY:
             finish_prompt(h)
 
@@ -411,9 +424,15 @@
 
     for c in kv:
         c.wait_send()
-    for i in range(1, 2 * NT):
-        for h in range(NPC):
-            prompt_copy(i // NT, i % NT, h).wait_send()
+    for h in range(NPC):
+        for a in range(1, NT):
+            prompt_copy(0, a, h).wait_send()
+
+        @pl.when(side == 0)
+        def _():
+            for a in range(NT):
+                prompt_copy(1, a, h).wait_send()
+
     for a in range(1, NT):
         resp_copy(a).wait_send()
     for piece in range(NPC, -1, -1):
@@ -426,6 +445,7 @@
 
 def per_device(queries, keys, values, dout, offsets, lengths):
     V = pl.BlockSpec(memory_space=pltpu.VMEM)
+    H = pl.BlockSpec(memory_space=pl.ANY)
     SM = pl.BlockSpec(memory_space=pltpu.SMEM)
     D = pltpu.SemaphoreType.DMA
     big = pltpu.VMEM((KEYS // 128, BQ, 128), f32)
@@ -435,7 +455,7 @@
         pl.pallas_call(
             kernel,
             out_shape=[jax.ShapeDtypeStruct((ROWS, DH), bf)] * 3,
-            in_specs=[SM, SM, V, V, V, V],
+            in_specs=[SM, SM, H, H, H, H],
             out_specs=[V, V, V],
             scratch_shapes=[
                 pltpu.VMEM((KEYS, DH), bf), pltpu.VMEM((KEYS, DH), bf),
@@ -448,7 +468,7 @@
                 pltpu.VMEM((2 * DH, KEYS), bf), pltpu.VMEM((2 * NT, FT, PH), bf),
                 pltpu.VMEM((NT, FT, R), bf), pltpu.VMEM((2 * DH, ROWS), bf),
                 D((4,)), D((4,)), D((NPC, 2 * NT)), D((NPC, 2 * NT)), D((NT,)), D((NT,)),
-                D((NPC + 1, NT)), D((NPC + 1, NT)), D((3,)), D((3,)),
+                D((NPC + 1, NT)), D((NPC + 1, NT)), D((3,)), D((3,)), D((6,)),
             ],
             compiler_params=pltpu.CompilerParams(
                 collective_id=0, has_side_effects=True, vmem_limit_bytes=60 * 2**20

time: 113 us -> 111 us (0.982)
  Pallas kernels: 107 us -> 105 us
    pallas_call x1, Pallas kernels: 107 us -> 105 us  [per_device(): pl.pallas_call(kernel, out_shape=[jax.ShapeDtypeStruct((ROWS, DH), bf)] *...]
where the time goes in v1:
time: 111 us; the launch traced here: 110 us
  Pallas kernels  105 us (95%)
  local copies, waits for them, and re-layouts  4.44 us (4%)
  between operations  1.3 us (1%)
    pallas_call x1, Pallas kernels, per_device(): pl.pallas_call(kernel, out_shape=[jax.ShapeDtypeStruct((ROWS, DH), bf)] *...  105 us
    unnamed x7, local copies, waits for them, and re-layouts  4.44 us

profile of v1, /device:TPU:0, one launch (start us, length us, event | category | flops | bytes accessed | tf_op | source)
XLA Modules:
  0.0 110.4 jit_solution(10194492999250990102)
XLA Ops:
  1.3 104.6 %shard_map.85 = (bf16[3072,128]{1,0:T(8,128)(2,1)}, bf16[3072,128]{1,0:T(8,128)(2,1)}, bf16[3072,128]{1,0:T(8,128)(2,1)}) custom-call(s32[8]{0:T(128)} %offs.1, s32[1]{0:T(128)S(6)} %copy.12.lens, bf16[3072,128]{1,0:T(8,128)(2,1)} %q.1, bf16[3072,128]{1,0:T(8,128)(2,1)} %kin.1, bf16[3072,128]{1,0:T(8,128)(2,1)} %vin.1, bf16[3072,128]{1,0:T(8,128)(2,1)} %do.1), custom_call_target="tpu_custom_call" | custom-call | tf_op jit(solution)/shard_map/pallas_call | solution.py:455
  105.9 0.0 copy-start.1
  105.9 2.1 %copy.13 = bf16[3072,128]{1,0:T(8,128)(2,1)} copy(bf16[3072,128]{1,0:T(8,128)(2,1)} %get-tuple-element.6) | data formatting | bytes 1572864
  108.1 0.0 copy-done.1
  108.1 0.0 copy-start
  108.1 0.9 copy.14
  109.0 0.5 copy-done
  109.5 0.9 copy.15
Async XLA Ops:
  105.9 2.1 %copy-start.1 = (bf16[3072,128]{1,0:T(8,128)(2,1)S(1)}, bf16[3072,128]{1,0:T(8,128)(2,1)}, u32[]{:S(2)}) copy-start(bf16[3072,128]{1,0:T(8,128)(2,1)} %get-tuple-element.7) | copy-start | bytes 2359300
  108.1 1.4 %copy-start = (bf16[3072,128]{1,0:T(8,128)(2,1)S(1)}, bf16[3072,128]{1,0:T(8,128)(2,1)}, u32[]{:S(2)}) copy-start(bf16[3072,128]{1,0:T(8,128)(2,1)} %get-tuple-element.8) | copy-start | bytes 2359300

commit v2 on v1

--- a/solution.py
+++ b/solution.py
@@ -16,7 +16,7 @@
 DH = 128
 KEYS = 2 * PH + R
 BQ, BK = 256, 512
-RG = 16
+RG = 32
 T = BK // 128
 NT = 8
 FT = 2 * DH // NT
@@ -26,7 +26,7 @@
 XR = 768
 ROWS = PH + R
 NEG = -1e30
-EARLY = (3,)
+EARLY = ()
 SCALE = 1.0 / DH**0.5
 CC = SCALE * 1.4426950408889634
 
@@ -99,11 +99,6 @@
         send_sem=x_s.at[2], recv_sem=x_r.at[2], device_id=peer(1, 0), device_id_type=MESH,
     )
 
-    @pl.when(side == 1)
-    def _():
-        for c in over:
-            c.start()
-
     kp = lax.broadcasted_iota(jnp.int32, (8, KEYS), 1)
     bias[...] = jnp.where(kp >= offset, 0.0, NEG).astype(f32)
     dkT[...] = jnp.zeros_like(dkT)
@@ -131,7 +126,7 @@
     def ks(c):
         return pl.ds(pl.multiple_of(c * BK, BK), BK)
 
-    def scores(slot, row0, pos0, c, masked):
+    def scores(slot, row0, pos0, c, masked, padded=True):
         DP = DPS[slot]
         s = dot_nt(qa[pl.ds(row0, BQ), :], k[ks(c), :])
         dp = dot_nt(dom[pl.ds(row0, BQ), :], v[ks(c), :])
@@ -146,7 +141,7 @@
                     ct = cols + i * 128
                     ok = (ct < rows) & (ct + c * BK >= offset) | (ct == rows)
                     st = jnp.where(ok, st, NEG)
-                else:
+                elif padded:
                     st = st + bias[0:1, pl.ds(pl.multiple_of(c * BK + i * 128, 128), 128)]
                 S[c * T + i, r : r + RG, :] = st
                 m = jnp.maximum(m, st)
@@ -262,25 +257,31 @@
     def finish_resp():
         for a in range(1, NT):
             resp_copy(a).wait_recv()
-        for i in range(R // 128):
-            cols = slice(i * 128, (i + 1) * 128)
-            total = sb[feats(0), 2 * PH + i * 128 : 2 * PH + (i + 1) * 128].astype(f32)
+
+        def tile(c):
+            cols = pl.ds(pl.multiple_of(c * 128, 128), 128)
+            total = sb[feats(0), pl.ds(pl.multiple_of(2 * PH + c * 128, 128), 128)].astype(f32)
             for a in range(1, NT):
                 total = total + rr[a, :, cols].astype(f32)
-            ga[feats(0), PH + i * 128 : PH + (i + 1) * 128] = total.astype(bf)
+            ga[feats(0), pl.ds(pl.multiple_of(PH + c * 128, 128), 128)] = total.astype(bf)
+
+        loop(0, R // 128, tile)
         for a in range(1, NT):
             gather(NPC, a).start()
 
     def finish_prompt(h):
         for i in range(1, 2 * NT):
             prompt_copy(i // NT, i % NT, h).wait_recv()
-        for c in range(HT):
-            cols = slice(h * PC + c * 128, h * PC + (c + 1) * 128)
+
+        def tile(c):
+            cols = pl.ds(pl.multiple_of(h * PC + c * 128, 128), 128)
             mine = pl.ds(pl.multiple_of(side * PH + h * PC + c * 128, 128), 128)
             total = sb[feats(0), mine].astype(f32)
             for i in range(1, 2 * NT):
                 total = total + rb[i, :, cols].astype(f32)
             ga[feats(0), cols] = total.astype(bf)
+
+        loop(0, HT, tile)
         for a in range(1, NT):
             gather(h, a).start()
 
@@ -295,6 +296,14 @@
     scores(0, row_a, pos_a, na - 1, True)
     for c in kv:
         c.wait_recv()
+
+    @pl.when(side == 1)
+    def _():
+        for c in kv:
+            c.wait_send()
+        for c in over:
+            c.start()
+
     loop(PB - side * PB, 2 * PB - side * PB, lambda c: scores(0, row_a, pos_a, c, False))
     row_max()
 
@@ -314,10 +323,10 @@
         r1, _, n1 = info(j + 1)
         r2, p2, n2 = info(j + 2)
 
-        def three(c, masked=False):
+        def three(c, masked=False, padded=True):
             p, x = grads_in(slot, c)
             expo(1 - slot, c)
-            scores(slot, r2, p2, c, masked)
+            scores(slot, r2, p2, c, masked, padded)
             grads_out(c, p, x)
 
         def two_of(c):
@@ -328,7 +337,8 @@
         def one_of(c):
             grads_out(c, *grads_in(slot, c))
 
-        loop(0, n2 - 1, three)
+        loop(0, jnp.minimum(n2 - 1, PH // BK), three)
+        loop(PH // BK, n2 - 1, lambda c: three(c, padded=False))
 
         @pl.when(n2 > 0)
         def _():
@@ -415,6 +425,8 @@
     @pl.when(side == 0)
     def _():
         back.wait_send()
+        for c in kv:
+            c.wait_send()
 
     @pl.when(side == 1)
     def _():
@@ -422,8 +434,6 @@
         for c in over:
             c.wait_send()
 
-    for c in kv:
-        c.wait_send()
     for h in range(NPC):
         for a in range(1, NT):
             prompt_copy(0, a, h).wait_send()

time: 111 us -> 111 us (level)
  no operation moved by 1% of the time
where the time goes in v2:
time: 111 us
  Pallas kernels  105 us (95%)
  local copies, waits for them, and re-layouts  4.44 us (4%)
  between operations  1.3 us (1%)
    pallas_call x1, Pallas kernels, per_device(): pl.pallas_call(kernel, out_shape=[jax.ShapeDtypeStruct((ROWS, DH), bf)] *...  105 us
    unnamed x7, local copies, waits for them, and re-layouts  4.44 us

profile of v2, /device:TPU:0, one launch (start us, length us, event | category | flops | bytes accessed | tf_op | source)
XLA Modules:
  0.0 110.6 jit_solution(13639081528134093560)
XLA Ops:
  1.3 104.8 %shard_map.85 = (bf16[3072,128]{1,0:T(8,128)(2,1)}, bf16[3072,128]{1,0:T(8,128)(2,1)}, bf16[3072,128]{1,0:T(8,128)(2,1)}) custom-call(s32[8]{0:T(128)} %offs.1, s32[1]{0:T(128)S(6)} %copy.12.lens, bf16[3072,128]{1,0:T(8,128)(2,1)} %q.1, bf16[3072,128]{1,0:T(8,128)(2,1)} %kin.1, bf16[3072,128]{1,0:T(8,128)(2,1)} %vin.1, bf16[3072,128]{1,0:T(8,128)(2,1)} %do.1), custom_call_target="tpu_custom_call" | custom-call | tf_op jit(solution)/shard_map/pallas_call | solution.py:465
  106.1 0.0 copy-start.1
  106.1 2.1 %copy.13 = bf16[3072,128]{1,0:T(8,128)(2,1)} copy(bf16[3072,128]{1,0:T(8,128)(2,1)} %get-tuple-element.6) | data formatting | bytes 1572864
  108.3 0.0 copy-done.1
  108.3 0.0 copy-start
  108.3 0.9 copy.14
  109.1 0.5 copy-done
  109.7 0.9 copy.15
Async XLA Ops:
  106.1 2.1 %copy-start.1 = (bf16[3072,128]{1,0:T(8,128)(2,1)S(1)}, bf16[3072,128]{1,0:T(8,128)(2,1)}, u32[]{:S(2)}) copy-start(bf16[3072,128]{1,0:T(8,128)(2,1)} %get-tuple-element.7) | copy-start | bytes 2359300
  108.3 1.4 %copy-start = (bf16[3072,128]{1,0:T(8,128)(2,1)S(1)}, bf16[3072,128]{1,0:T(8,128)(2,1)}, u32[]{:S(2)}) copy-start(bf16[3072,128]{1,0:T(8,128)(2,1)} %get-tuple-element.8) | copy-start | bytes 2359300
